TPU v7x, 128 devices: a whole 4x4x4 slice. The times are simulated.
128 devices in a mesh: island: 2 (over z_lo), fsdp: 32 (over y, x, z_hi), tensor: 2 (over core).
Axes of the slice: x: 4, y: 4, z: 4 (z_hi: 2, z_lo: 2; z = z_hi * 2 + z_lo), core: 2. Of those that a mesh axis runs over, the one named last changes fastest.
Arguments:
- activations: bfloat16 [65536, 8192], P(('island', 'fsdp'), 'tensor'), may hold values from -6 to 6
- cotangent: bfloat16 [65536, 2, 512], P(('island', 'fsdp'), None, 'tensor'), may hold values from -0.078125 to 0.078125
- inner_params: float32 [2, 8192, 2, 512], P('island', 'fsdp', None, 'tensor'), may hold values from -3 to 3
- first_moment: float32 [2, 8192, 2, 512], P('island', 'fsdp', None, 'tensor'), may hold values from -0.75 to 0.75
- second_moment: float32 [2, 8192, 2, 512], P('island', 'fsdp', None, 'tensor'), may hold values from 0.02 to 0.2
- global_params: float32 [8192, 2, 512], P('fsdp', None, 'tensor'), may hold values from -3 to 3
- outer_momentum: float32 [8192, 2, 512], P('fsdp', None, 'tensor'), may hold values from -1.5 to 1.5
Outputs:
- new_first: float32 [2, 8192, 2, 512], P('island', 'fsdp', None, 'tensor')
- new_second: float32 [2, 8192, 2, 512], P('island', 'fsdp', None, 'tensor')
- new_momentum: float32 [8192, 2, 512], P('fsdp', None, 'tensor')
- new_global: float32 [8192, 2, 512], P('fsdp', None, 'tensor')
- projected: bfloat16 [65536, 2, 512], P(('island', 'fsdp'), None, 'tensor')
All inputs are finite; a program needn't handle non-finite values.
Results may differ from a plain program's by a relative error of at most 0.0049.
Values may be sent and summed in bfloat16 or wider, within the bound.
A program may use at most 128 MiB of HBM per device.

v0:
```python
import jax
import jax.numpy as jnp
from jax import lax
from jax.sharding import PartitionSpec as P

D = 8192
STEP = 20


beta_one = 0.9
beta_two = 0.95
adam_eps = 1e-08
inner_rate = 0.05
weight_decay = 0.1
outer_rate = 0.7
outer_mu = 0.9


def contract_rows(features, right):
    return lax.dot_general(
        features, right, (((0,), (0,)), ((), ())), preferred_element_type=jnp.float32
    )


def shards(
    activations, cotangent, inner_params, first_moment, second_moment, global_params, outer_momentum
):
    columns = lax.all_gather(activations, "tensor", axis=1, tiled=True)
    tok_rows = columns.shape[0]
    kv_local = cotangent.shape[2]
    own_rows = inner_params.shape[1]
    flat_cot = cotangent.reshape(tok_rows, 2 * kv_local)
    grad = lax.psum_scatter(
        contract_rows(columns, flat_cot).reshape(lax.axis_size("fsdp") * own_rows, 2, kv_local),
        "fsdp",
        scatter_dimension=0,
        tiled=True,
    )
    theta = inner_params[0]
    new_first = beta_one * first_moment[0] + (1.0 - beta_one) * grad
    new_second = beta_two * second_moment[0] + (1.0 - beta_two) * grad * grad
    ascent = (
        new_first
        / (1.0 - beta_one**STEP)
        / (jnp.sqrt(new_second / (1.0 - beta_two**STEP)) + adam_eps)
    )
    inner = theta - inner_rate * (ascent + weight_decay * theta)
    difference = global_params - inner
    replicas = lax.axis_size("island")
    delta = lax.psum(difference, "island") / replicas
    new_momentum = outer_mu * outer_momentum + delta
    new_global = global_params - outer_rate * (delta + outer_mu * new_momentum)
    weights = new_global.astype(jnp.bfloat16)
    piece = lax.all_gather(weights, "fsdp", axis=0, tiled=True)
    flat = piece.reshape(piece.shape[0], 2 * kv_local)
    product = jnp.dot(columns, flat, preferred_element_type=jnp.float32)
    projected = (product * D ** (-0.5)).reshape(tok_rows, 2, kv_local).astype(jnp.bfloat16)
    return (new_first[None], new_second[None], new_momentum, new_global, projected)


def solution(mesh):
    in_specs = (
        P(("island", "fsdp"), "tensor"),
        P(("island", "fsdp"), None, "tensor"),
        P("island", "fsdp", None, "tensor"),
        P("island", "fsdp", None, "tensor"),
        P("island", "fsdp", None, "tensor"),
        P("fsdp", None, "tensor"),
        P("fsdp", None, "tensor"),
    )
    out_specs = (
        P("island", "fsdp", None, "tensor"),
        P("island", "fsdp", None, "tensor"),
        P("fsdp", None, "tensor"),
        P("fsdp", None, "tensor"),
        P(("island", "fsdp"), None, "tensor"),
    )
    return jax.shard_map(shards, mesh=mesh, in_specs=in_specs, out_specs=out_specs, check_vma=False)
```

profile of v0, /device:TPU:0, one launch (start us, length us, event | category | flops | bytes accessed | tf_op | source)
XLA Modules:
  0.0 618.6 jit_solution(8791753124686099572)
XLA Ops:
  7.2 0.0 all-gather.3.cloned.1.call-start
  7.2 12.0 %copy.26 = bf16[1024,4096]{0,1:T(8,128)(2,1)} copy(bf16[1024,4096]{1,0:T(8,128)(2,1)} %param.7) | data formatting | bytes 16777216 | tf_op args[0]
  19.2 0.0 copy-start.1
  19.2 0.0 all-gather.3.cloned.1.call-update
  19.2 0.0 reduce-scatter.2.cloned.1.call-start
  19.3 1.1 copy-done.1
  20.4 0.2 copy.39
  20.7 0.5 copy.27
  21.2 33.4 %all-gather.3.cloned.1.call-done = bf16[1024,8192]{0,1:T(8,128)(2,1)} async-done(((bf16[1024,4096]{0,1:T(8,128)(2,1)}), bf16[1024,8192]{0,1:T(8,128)(2,1)}) %all-gather.3.cloned.1.call-update) | async-done | bytes 16777232 | tf_op jit(solution)/shard_map/all_gather | solution.py:28
  54.6 15.7 %fusion = f32[8192,2,256]{2,0,1:T(8,128)} fusion(bf16[2,256,1024]{2,1,0:T(8,128)(2,1)S(1)} %bitcast.45, bf16[1024,8192]{0,1:T(8,128)(2,1)} %all-gather.3.cloned.1.call-done), kind=kOutput, calls=%fused_computation | convolution fusion | flops 8589934592 | bytes 34603008 | tf_op jit(solution)/shard_map/dot_general | solution.py:20
  70.3 0.0 copy-start
  70.3 0.0 copy-start.3
  70.3 0.0 copy-start.4
  70.3 0.0 copy-start.2
  70.3 0.0 reduce-scatter.2.cloned.1.call-update
  70.4 0.0 all-reduce.2.cloned.1.call-start
  70.4 364.1 %reduce-scatter.2.cloned.1.call-done = f32[256,2,256]{2,0,1:T(8,128)} async-done(((f32[8192,2,256]{2,0,1:T(8,128)}), f32[256,2,256]{2,0,1:T(8,128)}) %reduce-scatter.2.cloned.1.call-update) | async-done | bytes 524304 | tf_op jit(solution)/shard_map/reduce_scatter | solution.py:33
  434.5 0.0 copy-done
  434.5 0.0 copy-done.3
  434.5 0.0 copy-done.4
  434.5 2.4 fusion.5
  436.9 0.0 all-reduce.2.cloned.1.call-update
  437.0 0.0 all-gather.5.cloned.1.call-start
  437.0 36.3 %all-reduce.2.cloned.1.call-done = f32[256,2,256]{2,0,1:T(8,128)} async-done(((f32[256,2,256]{2,0,1:T(8,128)}), f32[256,2,256]{2,0,1:T(8,128)}) %all-reduce.2.cloned.1.call-update) | async-done | bytes 524304 | tf_op jit(solution)/shard_map/psum | solution.py:50
  473.3 0.0 copy-done.2
  473.3 1.9 fusion.9
  475.2 0.0 all-gather.5.cloned.1.call-update
  475.2 1.2 copy.35
  476.4 1.2 copy.34
  477.6 1.2 copy.37
  478.8 1.2 copy.36
  480.0 103.3 %all-gather.5.cloned.1.call-done = bf16[8192,2,256]{2,0,1:T(8,128)(2,1)} async-done(((bf16[256,2,256]{2,0,1:T(8,128)(2,1)}), bf16[8192,2,256]{2,0,1:T(8,128)(2,1)}) %all-gather.5.cloned.1.call-update) | async-done | bytes 8388624 | tf_op jit(solution)/shard_map/all_gather | solution.py:54
  583.3 11.9 %copy.33 = bf16[8192,2,256]{0,2,1:T(8,128)(2,1)} copy(bf16[8192,2,256]{2,0,1:T(8,128)(2,1)} %all-gather.5.cloned.1.call-done) | data formatting | bytes 16777216 | tf_op jit(solution)/shard_map/all_gather | solution.py:54
  595.2 14.8 %multiply_convert_fusion = bf16[512,1024]{1,0:T(8,128)(2,1)S(1)} fusion(bf16[8192,512]{0,1:T(8,128)(2,1)} %bitcast.42, bf16[1024,8192]{0,1:T(8,128)(2,1)} %all-gather.3.cloned.1.call-done), kind=kOutput, calls=%fused_computation.2 | convolution fusion | flops 8590983168 | bytes 26214400 | tf_op jit(solution)/shard_map/dot_general | solution.py:56
  610.0 2.0 copy.38
Async XLA Ops:
  7.2 47.4 %all-gather.3.cloned.1.call-start = ((), (), s32[]{:S(2)}) async-start(), calls=%async_computation.1 | async-start | bytes 25165824 | tf_op jit(solution)/shard_map/all_gather | solution.py:28
  19.2 1.2 copy-start.1
  19.2 415.3 %reduce-scatter.2.cloned.1.call-start = ((), (), s32[]{:S(2)}) async-start(), calls=%async_computation.2 | async-start | bytes 17301504 | tf_op jit(solution)/shard_map/reduce_scatter | solution.py:33
  70.3 364.2 %copy-start = (f32[256,2,256]{2,1,0:T(2,128)S(1)}, f32[256,2,256]{2,1,0:T(2,128)}, u32[]{:S(2)}) copy-start(f32[256,2,256]{2,1,0:T(2,128)} %param.12) | copy-start | bytes 1572868
  70.3 364.2 %copy-start.3 = (f32[1,256,2,256]{3,2,1,0:T(2,128)S(1)}, f32[1,256,2,256]{3,2,1,0:T(2,128)}, u32[]{:S(2)}) copy-start(f32[1,256,2,256]{3,2,1,0:T(2,128)} %param.9) | copy-start | bytes 1572868
  70.3 364.2 %copy-start.4 = (f32[1,256,2,256]{3,2,1,0:T(2,128)S(1)}, f32[1,256,2,256]{3,2,1,0:T(2,128)}, u32[]{:S(2)}) copy-start(f32[1,256,2,256]{3,2,1,0:T(2,128)} %param.10) | copy-start | bytes 1572868
  70.3 403.0 %copy-start.2 = (f32[256,2,256]{2,1,0:T(2,128)S(1)}, f32[256,2,256]{2,1,0:T(2,128)}, u32[]{:S(2)}) copy-start(f32[256,2,256]{2,1,0:T(2,128)} %param.13) | copy-start | bytes 1572868
  70.4 402.9 %all-reduce.2.cloned.1.call-start = ((), (), s32[]{:S(2)}) async-start(), calls=%async_computation.3 | async-start | bytes 1048576 | tf_op jit(solution)/shard_map/psum | solution.py:50
  437.0 146.4 %all-gather.5.cloned.1.call-start = ((), (), s32[]{:S(2)}) async-start(), calls=%async_computation.4 | async-start | bytes 8650752 | tf_op jit(solution)/shard_map/all_gather | solution.py:54
Sparse Core Ops, SparseCore 0:
  19.4 35.1 all-gather.2
  70.5 363.9 reduce-scatter.1
  437.5 35.7 all-reduce.1
  477.3 105.9 all-gather.4
where the time goes:
time: 620 us; the launch traced here: 619 us
  waiting for transfers between devices  537 us (87%)
  local copies, waits for them, and re-layouts  32.7 us (5%)
  matrix products  30.5 us (5%)
  between operations  13.8 us (2%)
    reduce_scatter x1, waiting for transfers between devices, shards(): lax.psum_scatter(contract_rows(columns, flat_cot).reshape(lax.axis_size('...  364 us
    all_gather x1, waiting for transfers between devices, shards(): piece = lax.all_gather(weights, 'fsdp', axis=0, tiled=True)  103 us
    psum x1, waiting for transfers between devices, shards(): delta = lax.psum(difference, 'island') / replicas  36.3 us
    all_gather x1, waiting for transfers between devices, shards(): columns = lax.all_gather(activations, 'tensor', axis=1, tiled=True)  33.4 us
    unnamed x17, local copies, waits for them, and re-layouts  20.2 us
    dot_general x1, matrix products, contract_rows(): lax.dot_general(features, right, (((0,), (0,)), ((), ())), preferred_elem...  15.7 us
    dot_general x1, matrix products, shards(): product = jnp.dot(columns, flat, preferred_element_type=jnp.float32)  14.8 us
  transfers between devices with their start and end apart: 4, of which 4 were waited for; matrix products, arithmetic and copies ran while one was open for 1% of the time, Pallas kernels for 0%

commit v1 on v0

v1 whole, which is shorter than its diff:
```python
import jax
import jax.numpy as jnp
from jax import lax
from jax.experimental import pallas as pl
from jax.experimental.pallas import tpu as pltpu
from jax.sharding import PartitionSpec as P

D = 8192
STEP = 20
beta_one = 0.9
beta_two = 0.95
adam_eps = 1e-08
inner_rate = 0.05
weight_decay = 0.1
outer_rate = 0.7
outer_mu = 0.9

MESH = pl.DeviceIdType.MESH
bf16 = jnp.bfloat16
f32 = jnp.float32

ORDER = [
    (2, 2), (2, 1), (1, 2), (2, 3), (3, 2), (1, 1), (3, 3), (1, 3),
    (3, 1), (0, 2), (2, 0), (0, 1), (1, 0), (0, 3), (3, 0), (0, 0),
]
ARRIVAL = [
    (0, 0), (0, 1), (1, 0), (0, 3), (3, 0), (0, 2), (2, 0), (1, 1),
    (3, 3), (1, 3), (3, 1), (1, 2), (2, 1), (3, 2), (2, 3), (2, 2),
]


class Numbers:
    def __init__(self):
        self.of = {}

    def __call__(self, key):
        return self.of.setdefault(key, len(self.of))


def kernel(
    count, x_hbm, ct, m_ref, v_ref, th_ref, gp_ref, om_ref,
    nf, ns, nm, ng, out,
    Xc, Pt, A2, Ap, Am, B2, Bp, Bm, Zs, Zr, F, W, Ts, Tr, As, Ar, acc,
    lsem, ssem, rsem,
):
    i = lax.axis_index("island")
    f = lax.axis_index("fsdp")
    t = lax.axis_index("tensor")
    hme = lax.rem(f, 2)
    oh = 1 - hme
    x = lax.rem(lax.div(f, 2), 4)
    y = lax.div(f, 8)

    def wrap(v):
        return lax.rem(v, 4)

    def dev(xx, yy, hh, ii, tt):
        return {"island": ii, "fsdp": (yy * 4 + xx) * 2 + hh, "tensor": tt}

    peer = dev(x, y, hme, i, 1 - t)
    zfar = dev(x, y, oh, i, t)
    zisl = dev(x, y, hme, 1 - i, t)
    zmir = dev(x, y, oh, 1 - i, t)

    def near(axis, s):
        if axis == 0:
            return dev(wrap(x + s), y, hme, i, t)
        return dev(x, wrap(y + s), hme, i, t)

    numbers = Numbers()
    sent = []
    waited = set()

    def message(key, src, dst, to):
        n = numbers(key)
        return pltpu.make_async_remote_copy(
            src_ref=src, dst_ref=dst, send_sem=ssem.at[n], recv_sem=rsem.at[n],
            device_id=to, device_id_type=MESH,
        )

    def send(key, src, dst, to):
        message(key, src, dst, to).start()
        sent.append((key, src, dst, to))

    def recv(key, dst):
        if key not in waited:
            waited.add(key)
            message(key, dst, dst, peer).wait_recv()

    barrier = pltpu.get_barrier_semaphore()
    friends = [near(0, 1), near(0, 3), near(1, 1), near(1, 3), peer, zfar, zisl, zmir]
    for d in friends:
        pl.semaphore_signal(barrier, inc=1, device_id=d, device_id_type=MESH)

    def place(p, ja, jb):
        dx, dy = (ja, jb) if p == 0 else (jb, ja)
        return wrap(y + dy), wrap(x + dx)

    def chunk(c):
        dy, dx = ORDER[c]
        yy, xx = wrap(y + dy), wrap(x + dx)
        k = yy * 4 + xx
        mine = lax.div(yy, 2) == t
        src = x_hbm.at[:, pl.ds(pl.multiple_of(lax.rem(k, 8) * 512, 512), 512)]
        return k, mine, src

    for c in range(16):
        k, mine, src = chunk(c)

        @pl.when(mine)
        def _():
            pltpu.make_async_copy(src, Xc.at[k], lsem.at[c]).start()

    pl.semaphore_wait(barrier, len(friends))
    for c in range(16):
        k, mine, src = chunk(c)
        n = numbers(("X", c))

        @pl.when(mine)
        def _():
            message(("X", c), src, Xc.at[k], peer).start()

    def gradient(c):
        k, mine, src = chunk(c)

        @pl.when(mine)
        def _():
            pltpu.make_async_copy(src, Xc.at[k], lsem.at[c]).wait()

        @pl.when(jnp.logical_not(mine))
        def _():
            message(("X", c), Xc.at[k], Xc.at[k], peer).wait_recv()

        dy, dx = ORDER[c]
        yy, xx = wrap(y + dy), wrap(x + dx)
        for h in range(2):
            part = jnp.dot(
                ct[...], Xc[k, :, h * 256 : (h + 1) * 256], preferred_element_type=f32
            ).astype(bf16)
            for u in range(2):
                for p in range(2):
                    r = (u * 2 + p) * 128
                    Pt[u, p, yy, xx, h] = part[r : r + 128]

    def Pc(u, p, ja, jb, h):
        yy, xx = place(p, ja, jb)
        return Pt.at[u, p, yy, xx, h]

    def first_sends(u, c):
        dy, dx = ORDER[c]
        for p in range(2):
            a = p
            ja, jb = (dx, dy) if p == 0 else (dy, dx)
            if ja == 2:
                send(("A2", u, p, jb, 0), Pc(u, p, 2, jb, 0), A2.at[u, p, jb, 0], near(a, 1))
                send(("A2", u, p, jb, 1), Pc(u, p, 2, jb, 1), A2.at[u, p, jb, 1], near(a, 3))
            elif ja == 1:
                send(("Am", u, p, jb, 1), Pc(u, p, 1, jb, 1), Am.at[u, p, jb, 1], near(a, 1))
            elif ja == 3:
                send(("Ap", u, p, jb, 0), Pc(u, p, 3, jb, 0), Ap.at[u, p, jb, 0], near(a, 3))

    def add_to(dst, src):
        dst[...] = (dst[...].astype(f32) + src[...].astype(f32)).astype(bf16)

    def rs1b(u, jb):
        for p in range(2):
            a = p
            recv(("A2", u, p, jb, 0), A2.at[u, p, jb, 0])
            add_to(Pc(u, p, 1, jb, 0), A2.at[u, p, jb, 0])
            send(("Am", u, p, jb, 0), Pc(u, p, 1, jb, 0), Am.at[u, p, jb, 0], near(a, 1))
            recv(("A2", u, p, jb, 1), A2.at[u, p, jb, 1])
            add_to(Pc(u, p, 3, jb, 1), A2.at[u, p, jb, 1])
            send(("Ap", u, p, jb, 1), Pc(u, p, 3, jb, 1), Ap.at[u, p, jb, 1], near(a, 3))

    def rs1c(u, jb):
        for p in range(2):
            b = 1 - p
            for h in range(2):
                recv(("Am", u, p, jb, h), Am.at[u, p, jb, h])
                recv(("Ap", u, p, jb, h), Ap.at[u, p, jb, h])
                own = Pc(u, p, 0, jb, h)
                s = own[...].astype(f32) + Am[u, p, jb, h].astype(f32) + Ap[u, p, jb, h].astype(f32)
                if jb == 0:
                    F[u, p, h] = s
                else:
                    own[...] = s.astype(bf16)
                    if jb == 2:
                        send(("B2", u, p, h), own, B2.at[u, p, h], near(b, 1 if h == 0 else 3))
                    elif jb == 1 and h == 1:
                        send(("Bm", u, p, 1), own, Bm.at[u, p, 1], near(b, 1))
                    elif jb == 3 and h == 0:
                        send(("Bp", u, p, 0), own, Bp.at[u, p, 0], near(b, 3))

    def rs2b(u):
        for p in range(2):
            b = 1 - p
            recv(("B2", u, p, 0), B2.at[u, p, 0])
            add_to(Pc(u, p, 0, 1, 0), B2.at[u, p, 0])
            send(("Bm", u, p, 0), Pc(u, p, 0, 1, 0), Bm.at[u, p, 0], near(b, 1))
            recv(("B2", u, p, 1), B2.at[u, p, 1])
            add_to(Pc(u, p, 0, 3, 1), B2.at[u, p, 1])
            send(("Bp", u, p, 1), Pc(u, p, 0, 3, 1), Bp.at[u, p, 1], near(b, 3))

    def rs2c(u):
        for p in range(2):
            for h in range(2):
                recv(("Bm", u, p, h), Bm.at[u, p, h])
                recv(("Bp", u, p, h), Bp.at[u, p, h])
                F[u, p, h] += Bm[u, p, h].astype(f32) + Bp[u, p, h].astype(f32)
            Zs[u, p] = F[u, p, oh].astype(bf16)
            send(("Z", u, p), Zs.at[u, p], Zr.at[u, p], zfar)

    def start_islands():
        for u in range(2):
            th = th_ref[:, u, :]
            Ts[u] = gp_ref[:, u, :] - (th - (inner_rate * weight_decay) * th)
        send(("T",), Ts, Tr, zisl)

    def adam(u):
        for p in range(2):
            cols = slice(p * 128, (p + 1) * 128)
            recv(("Z", u, p), Zr.at[u, p])
            grad = (F[u, p, hme] + Zr[u, p].astype(f32)).T
            first = beta_one * m_ref[:, u, cols] + (1.0 - beta_one) * grad
            second = beta_two * v_ref[:, u, cols] + (1.0 - beta_two) * grad * grad
            nf[:, u, cols] = first
            ns[:, u, cols] = second
            ascent = (
                first / (1.0 - beta_one**STEP)
                / (jnp.sqrt(second / (1.0 - beta_two**STEP)) + adam_eps)
            )
            As[u, p] = ascent.astype(bf16)
            send(("I", u, p), As.at[u, p], Ar.at[u, p], zisl)

    def Wp(u, p, ja, jb):
        yy, xx = place(p, ja, jb)
        return W.at[u, yy, xx, :, p]

    def Wh(u, p, ja, jb, h):
        yy, xx = place(p, ja, jb)
        return W.at[u, yy, xx, h, p]

    def outer(u):
        recv(("T",), Tr)
        for p in range(2):
            cols = slice(p * 128, (p + 1) * 128)
            recv(("I", u, p), Ar.at[u, p])
            steps = As[u, p].astype(f32) + Ar[u, p].astype(f32)
            delta = ((Ts[u, :, cols] + Tr[u, :, cols]) + inner_rate * steps) * 0.5
            momentum = outer_mu * om_ref[:, u, cols] + delta
            fresh = gp_ref[:, u, cols] - outer_rate * (delta + outer_mu * momentum)
            nm[:, u, cols] = momentum
            ng[:, u, cols] = fresh
            low = fresh.astype(bf16)
            W[u, y, x, hme, 0, :, cols] = low[:128]
            W[u, y, x, hme, 1, :, cols] = low[128:]
        send(("Gz", u), W.at[u, y, x, hme], W.at[u, y, x, hme], zmir)
        spread(u, 0)

    def spread(u, s):
        h = hme if s == 0 else oh
        for p in range(2):
            for g in (1, 3):
                ref = Wh(u, p, 0, 0, h)
                send(("G1", u, p, s, g), ref, ref, near(p, g))
                send(("G2", u, p, 0, s, g), ref, ref, near(1 - p, g))

    def agz(u):
        recv(("Gz", u), W.at[u, y, x, oh])
        spread(u, 1)

    def g2(u, p, j):
        for g in (1, 3):
            ref = Wp(u, p, j, 0)
            send(("G2", u, p, j, g), ref, ref, near(1 - p, g))

    def ag1(u):
        for p in range(2):
            recv(("G1", u, p, 0, 1), Wh(u, p, 3, 0, hme))
            ref = Wh(u, p, 3, 0, hme)
            send(("G1f", u, p, 1), ref, ref, near(p, 1))
            recv(("G1", u, p, 1, 3), Wh(u, p, 1, 0, oh))
            ref = Wh(u, p, 1, 0, oh)
            send(("G1f", u, p, 3), ref, ref, near(p, 3))
        for p in range(2):
            recv(("G1", u, p, 1, 1), Wh(u, p, 3, 0, oh))
            g2(u, p, 3)
            recv(("G1", u, p, 0, 3), Wh(u, p, 1, 0, hme))
            g2(u, p, 1)

    def ag1f(u):
        for p in range(2):
            recv(("G1f", u, p, 1), Wh(u, p, 2, 0, hme))
            recv(("G1f", u, p, 3), Wh(u, p, 2, 0, oh))
            g2(u, p, 2)

    def ag2f(u, j):
        for p in range(2):
            if j == 0:
                recv(("G2", u, p, 0, 0, 1), Wh(u, p, 0, 3, hme))
            else:
                recv(("G2", u, p, j, 1), Wp(u, p, j, 3))
            ref = Wh(u, p, j, 3, hme)
            send(("G2f", u, p, j, 1), ref, ref, near(1 - p, 1))
            if j == 0:
                recv(("G2", u, p, 0, 1, 3), Wh(u, p, 0, 1, oh))
            else:
                recv(("G2", u, p, j, 3), Wp(u, p, j, 1))
            ref = Wh(u, p, j, 1, oh)
            send(("G2f", u, p, j, 3), ref, ref, near(1 - p, 3))

    seen = set()

    def project(u, c):
        dy, dx = ARRIVAL[c]
        for p in range(2):
            ja, jb = (dx, dy) if p == 0 else (dy, dx)
            if jb == 3 and ja == 0:
                recv(("G2", u, p, 0, 1, 1), Wh(u, p, 0, 3, oh))
            if jb == 1 and ja == 0:
                recv(("G2", u, p, 0, 0, 3), Wh(u, p, 0, 1, hme))
            if jb == 2:
                recv(("G2f", u, p, ja, 1), Wh(u, p, ja, 2, hme))
                recv(("G2f", u, p, ja, 3), Wh(u, p, ja, 2, oh))
        yy, xx = wrap(y + dy), wrap(x + dx)
        right = W[u, yy, xx].reshape(512, 256)
        part = jnp.dot(Xc[yy * 4 + xx], right, preferred_element_type=f32)
        cols = slice(u * 256, (u + 1) * 256)
        if u not in seen:
            seen.add(u)
            acc[:, cols] = part
        elif c < 15:
            acc[:, cols] += part
        else:
            out[:, cols] = ((acc[:, cols] + part) * D ** (-0.5)).astype(bf16)

    for c in range(16):
        gradient(c)
        first_sends(0, c)
        if c == 6:
            start_islands()
    for q, jb in enumerate((2, 1, 3, 0)):
        rs1b(0, jb)
        for c in range(4 * q, 4 * q + 4):
            first_sends(1, c)
    for jb in (2, 1, 3, 0):
        rs1c(0, jb)
    rs2b(0)
    rs1b(1, 2)
    rs2c(0)
    rs1b(1, 1)
    adam(0)
    rs1b(1, 3)
    rs1b(1, 0)
    outer(0)
    rs1c(1, 2)
    agz(0)
    rs1c(1, 1)
    ag1(0)
    rs1c(1, 3)
    ag1f(0)
    rs1c(1, 0)
    ag2f(0, 0)
    rs2b(1)
    ag2f(0, 3)
    rs2c(1)
    ag2f(0, 1)
    adam(1)
    ag2f(0, 2)
    outer(1)
    for c in range(0, 5):
        project(0, c)
    agz(1)
    for c in range(5, 9):
        project(0, c)
    ag1(1)
    for c in range(9, 12):
        project(0, c)
    ag1f(1)
    for c in range(12, 16):
        project(0, c)
    ag2f(1, 0)
    project(1, 0)
    project(1, 1)
    ag2f(1, 3)
    project(1, 2)
    project(1, 3)
    ag2f(1, 1)
    project(1, 4)
    ag2f(1, 2)
    for c in range(5, 16):
        project(1, c)

    for key, src, dst, to in sent:
        message(key, src, dst, to).wait_send()
    for c in range(16):
        k, mine, src = chunk(c)

        @pl.when(mine)
        def _():
            message(("X", c), src, Xc.at[k], peer).wait_send()

    if len(numbers.of) != count:
        raise ValueError(len(numbers.of))


COUNT = 243


def shards(
    activations, cotangent, inner_params, first_moment, second_moment, global_params, outer_momentum
):
    tok, kv = cotangent.shape[0], cotangent.shape[2]
    rows = global_params.shape[0]
    ct = cotangent.reshape(tok, 2 * kv).T
    vmem = pl.BlockSpec(memory_space=pltpu.VMEM)
    state = jax.ShapeDtypeStruct((rows, 2, kv), f32)
    import functools

    piece = (128, 256)
    new_first, new_second, new_momentum, new_global, projected = pl.pallas_call(
        functools.partial(kernel, COUNT),
        out_shape=(state, state, state, state, jax.ShapeDtypeStruct((tok, 2 * kv), bf16)),
        in_specs=[pl.BlockSpec(memory_space=pl.ANY)] + [vmem] * 6,
        out_specs=(vmem,) * 5,
        scratch_shapes=[
            pltpu.VMEM((16, tok, 512), bf16),
            pltpu.VMEM((2, 2, 4, 4, 2) + piece, bf16),
            pltpu.VMEM((2, 2, 4, 2) + piece, bf16),
            pltpu.VMEM((2, 2, 4, 2) + piece, bf16),
            pltpu.VMEM((2, 2, 4, 2) + piece, bf16),
            pltpu.VMEM((2, 2, 2) + piece, bf16),
            pltpu.VMEM((2, 2, 2) + piece, bf16),
            pltpu.VMEM((2, 2, 2) + piece, bf16),
            pltpu.VMEM((2, 2) + piece, bf16),
            pltpu.VMEM((2, 2) + piece, bf16),
            pltpu.VMEM((2, 2, 2) + piece, f32),
            pltpu.VMEM((2, 4, 4, 2, 2) + piece, bf16),
            pltpu.VMEM((2, rows, kv), f32),
            pltpu.VMEM((2, rows, kv), f32),
            pltpu.VMEM((2, 2, rows, kv // 2), bf16),
            pltpu.VMEM((2, 2, rows, kv // 2), bf16),
            pltpu.VMEM((tok, 2 * kv), f32),
            pltpu.SemaphoreType.DMA((16,)),
            pltpu.SemaphoreType.DMA((COUNT,)),
            pltpu.SemaphoreType.DMA((COUNT,)),
        ],
        compiler_params=pltpu.CompilerParams(
            collective_id=0, has_side_effects=True, vmem_limit_bytes=62 * 2**20
        ),
        cost_estimate=pl.CostEstimate(
            flops=17_200_000_000, bytes_accessed=16 * 2**20, transcendentals=0
        ),
        name="outer_step",
    )(
        activations, ct, first_moment[0], second_moment[0], inner_params[0],
        global_params, outer_momentum,
    )
    return (
        new_first[None], new_second[None], new_momentum, new_global,
        projected.reshape(tok, 2, kv),
    )


def solution(mesh):
    in_specs = (
        P(("island", "fsdp"), "tensor"),
        P(("island", "fsdp"), None, "tensor"),
        P("island", "fsdp", None, "tensor"),
        P("island", "fsdp", None, "tensor"),
        P("island", "fsdp", None, "tensor"),
        P("fsdp", None, "tensor"),
        P("fsdp", None, "tensor"),
    )
    out_specs = (
        P("island", "fsdp", None, "tensor"),
        P("island", "fsdp", None, "tensor"),
        P("fsdp", None, "tensor"),
        P("fsdp", None, "tensor"),
        P(("island", "fsdp"), None, "tensor"),
    )
    return jax.shard_map(shards, mesh=mesh, in_specs=in_specs, out_specs=out_specs, check_vma=False)
```

time: 620 us -> 142 us (0.23)
  waiting for transfers between devices: 537 us -> 0 us
  Pallas kernels: 0 us -> 127 us
  matrix products: 30.5 us -> 0 us
  local copies, waits for them, and re-layouts: 32.7 us -> 13.8 us
  between operations: 13.8 us -> 0.64 us
    reduce_scatter x1 -> x0, waiting for transfers between devices: 364 us -> none  [shards(): lax.psum_scatter(contract_rows(columns, flat_cot).reshape(lax.axis_size('...]
    all_gather x2 -> x0, waiting for transfers between devices: 137 us -> none  [the longest x1 103 us: shards(): piece = lax.all_gather(weights, 'fsdp', axis=0, tiled=True)]
    pallas_call x0 -> x1, Pallas kernels: none -> 127 us  [shards(): pl.pallas_call(functools.partial(kernel, COUNT), out_shape=(state, state,...]
    psum x1 -> x0, waiting for transfers between devices: 36.3 us -> none  [shards(): delta = lax.psum(difference, 'island') / replicas]
    dot_general x2 -> x0, matrix products: 30.5 us -> none  [the longest x1 15.7 us: contract_rows(): lax.dot_general(features, right, (((0,), (0,)), ((), ())), preferred_elem...]
    all_gather x1 -> x0, local copies, waits for them, and re-layouts: 11.9 us -> none  [shards(): piece = lax.all_gather(weights, 'fsdp', axis=0, tiled=True)]
    unnamed x17 -> x5, local copies, waits for them, and re-layouts: 20.2 us -> 11.7 us
  transfers between devices with their start and end apart: 4 -> 0, of which waited for: 4 -> 0; matrix products, arithmetic and copies ran while one was open for 1% -> 0% of each run, Pallas kernels for 0% -> 0%
where the time goes in v1:
time: 142 us
  Pallas kernels  127 us (89%)
  local copies, waits for them, and re-layouts  13.8 us (10%)
    pallas_call x1, Pallas kernels, shards(): pl.pallas_call(functools.partial(kernel, COUNT), out_shape=(state, state,...  127 us
    unnamed x5, local copies, waits for them, and re-layouts  11.7 us

profile of v1, /device:TPU:0, one launch (start us, length us, event | category | flops | bytes accessed | tf_op | source)
XLA Modules:
  0.0 141.8 jit_solution(9117835727576838765)
XLA Ops:
  0.6 3.7 %copy.12 = bf16[1024,2,256]{0,2,1:T(8,128)(2,1)} copy(bf16[1024,2,256]{2,1,0:T(2,128)(2,1)} %param.8) | data formatting | bytes 2097152 | tf_op args[1]
  4.3 127.3 %outer_step.1 = (f32[256,2,256]{2,1,0:T(2,128)}, f32[256,2,256]{2,1,0:T(2,128)}, f32[256,2,256]{2,1,0:T(2,128)}, f32[256,2,256]{2,1,0:T(2,128)}, bf16[1024,512]{1,0:T(8,128)(2,1)}) custom-call(bf16[1024,4096]{1,0:T(8,128)(2,1)} %x_hbm.1, bf16[512,1024]{1,0:T(8,128)(2,1)} %bitcast.8, f32[256,2,256]{2,1,0:T(2,128)} %bitcast.11, f32[256,2,256]{2,1,0:T(2,128)} %bitcast.12, ...), custom_call_target="tpu_custom_call" | custom-call | flops 17200001024 | bytes 16777216 | tf_op jit(solution)/shard_map/outer_step/pallas_call | solution.py:421
  131.6 2.1 %reshape.17 = bf16[1024,2,256]{2,1,0:T(2,128)(2,1)} reshape(bf16[1024,512]{1,0:T(8,128)(2,1)} %get-tuple-element.14) | data formatting | bytes 2097152 | tf_op jit(solution)/shard_map/reshape | solution.py:461
  133.7 2.0 %copy.17 = f32[1,256,2,256]{3,2,1,0:T(2,128)} copy(f32[1,256,2,256]{3,2,1,0:T(2,128)} %bitcast.10) | data formatting | bytes 1048576
  135.7 2.0 %copy.18 = f32[1,256,2,256]{3,2,1,0:T(2,128)} copy(f32[1,256,2,256]{3,2,1,0:T(2,128)} %bitcast.9) | data formatting | bytes 1048576
  137.7 2.0 %copy.19 = f32[256,2,256]{2,1,0:T(2,128)} copy(f32[256,2,256]{2,1,0:T(2,128)} %get-tuple-element.22) | data formatting | bytes 1048576
  139.7 2.0 %copy.20 = f32[256,2,256]{2,1,0:T(2,128)} copy(f32[256,2,256]{2,1,0:T(2,128)} %get-tuple-element.23) | data formatting | bytes 1048576

commit v2 on v1

--- a/solution.py
+++ b/solution.py
@@ -1,3 +1,5 @@
+import functools
+
 import jax
 import jax.numpy as jnp
 from jax import lax
@@ -38,8 +40,9 @@
 
 
 def kernel(
-    count, x_hbm, ct, m_ref, v_ref, th_ref, gp_ref, om_ref,
-    nf, ns, nm, ng, out,
+    count, x_hbm, c_hbm, m_hbm, v_hbm, th_hbm, gp_hbm, om_hbm,
+    nf_hbm, ns_hbm, nm_hbm, ng_hbm, out_hbm,
+    cot, ct, m_ref, v_ref, th_ref, gp_ref, om_ref, nf, ns, nm, ng, out,
     Xc, Pt, A2, Ap, Am, B2, Bp, Bm, Zs, Zr, F, W, Ts, Tr, As, Ar, acc,
     lsem, ssem, rsem,
 ):
@@ -62,6 +65,8 @@
     zisl = dev(x, y, hme, 1 - i, t)
     zmir = dev(x, y, oh, 1 - i, t)
 
+    sense = 1 + 2 * i
+
     def near(axis, s):
         if axis == 0:
             return dev(wrap(x + s), y, hme, i, t)
@@ -91,6 +96,15 @@
     friends = [near(0, 1), near(0, 3), near(1, 1), near(1, 3), peer, zfar, zisl, zmir]
     for d in friends:
         pl.semaphore_signal(barrier, inc=1, device_id=d, device_id_type=MESH)
+
+    state_in = [
+        pltpu.make_async_copy(a, b, lsem.at[16 + n])
+        for n, (a, b) in enumerate((
+            (c_hbm, cot), (th_hbm, th_ref), (gp_hbm, gp_ref),
+            (m_hbm, m_ref), (v_hbm, v_ref), (om_hbm, om_ref),
+        ))
+    ]
+    state_in[0].start()
 
     def place(p, ja, jb):
         dx, dy = (ja, jb) if p == 0 else (jb, ja)
@@ -110,6 +124,12 @@
         @pl.when(mine)
         def _():
             pltpu.make_async_copy(src, Xc.at[k], lsem.at[c]).start()
+
+    for copy in state_in[1:]:
+        copy.start()
+    state_in[0].wait()
+    for u in range(2):
+        ct[u * 256 : (u + 1) * 256, :] = cot[:, u, :].T
 
     pl.semaphore_wait(barrier, len(friends))
     for c in range(16):
@@ -211,6 +231,8 @@
             send(("Z", u, p), Zs.at[u, p], Zr.at[u, p], zfar)
 
     def start_islands():
+        for copy in state_in[1:]:
+            copy.wait()
         for u in range(2):
             th = th_ref[:, u, :]
             Ts[u] = gp_ref[:, u, :] - (th - (inner_rate * weight_decay) * th)
@@ -232,12 +254,18 @@
             As[u, p] = ascent.astype(bf16)
             send(("I", u, p), As.at[u, p], Ar.at[u, p], zisl)
 
+    def place_w(p, ja, jb):
+        return place(p, sense * ja, sense * jb)
+
+    def near_w(axis, g):
+        return near(axis, sense * g)
+
     def Wp(u, p, ja, jb):
-        yy, xx = place(p, ja, jb)
+        yy, xx = place_w(p, ja, jb)
         return W.at[u, yy, xx, :, p]
 
     def Wh(u, p, ja, jb, h):
-        yy, xx = place(p, ja, jb)
+        yy, xx = place_w(p, ja, jb)
         return W.at[u, yy, xx, h, p]
 
     def outer(u):
@@ -260,28 +288,37 @@
     def spread(u, s):
         h = hme if s == 0 else oh
         for p in range(2):
+            ref = Wh(u, p, 0, 0, h)
             for g in (1, 3):
-                ref = Wh(u, p, 0, 0, h)
-                send(("G1", u, p, s, g), ref, ref, near(p, g))
-                send(("G2", u, p, 0, s, g), ref, ref, near(1 - p, g))
+                send(("G1", u, p, s, g), ref, ref, near_w(p, g))
+            send(("G2b", u, p, 0, s), ref, ref, near_w(1 - p, 3))
+
+            @pl.when(h == i)
+            def _():
+                message(("G2e", u, p, 0), ref, ref, near_w(1 - p, 1)).start()
+
+            if s == 1:
+                own = Wh(u, p, 0, 0, i)
+                sent.append((("G2e", u, p, 0), own, own, near_w(1 - p, 1)))
 
     def agz(u):
         recv(("Gz", u), W.at[u, y, x, oh])
         spread(u, 1)
 
     def g2(u, p, j):
-        for g in (1, 3):
-            ref = Wp(u, p, j, 0)
-            send(("G2", u, p, j, g), ref, ref, near(1 - p, g))
+        ref = Wh(u, p, j, 0, i)
+        send(("G2e", u, p, j), ref, ref, near_w(1 - p, 1))
+        ref = Wp(u, p, j, 0)
+        send(("G2b", u, p, j), ref, ref, near_w(1 - p, 3))
 
     def ag1(u):
         for p in range(2):
-            recv(("G1", u, p, 0, 1), Wh(u, p, 3, 0, hme))
             ref = Wh(u, p, 3, 0, hme)
-            send(("G1f", u, p, 1), ref, ref, near(p, 1))
-            recv(("G1", u, p, 1, 3), Wh(u, p, 1, 0, oh))
+            recv(("G1", u, p, 0, 1), ref)
+            send(("G1f", u, p, 1), ref, ref, near_w(p, 1))
             ref = Wh(u, p, 1, 0, oh)
-            send(("G1f", u, p, 3), ref, ref, near(p, 3))
+            recv(("G1", u, p, 1, 3), ref)
+            send(("G1f", u, p, 3), ref, ref, near_w(p, 3))
         for p in range(2):
             recv(("G1", u, p, 1, 1), Wh(u, p, 3, 0, oh))
             g2(u, p, 3)
@@ -294,20 +331,35 @@
             recv(("G1f", u, p, 3), Wh(u, p, 2, 0, oh))
             g2(u, p, 2)
 
+    def ahead(u, p, j):
+        if j == 0:
+            recv(("G2b", u, p, 0, 0), Wh(u, p, 0, 1, hme))
+            recv(("G2b", u, p, 0, 1), Wh(u, p, 0, 1, oh))
+        else:
+            recv(("G2b", u, p, j), Wp(u, p, j, 1))
+
     def ag2f(u, j):
         for p in range(2):
-            if j == 0:
-                recv(("G2", u, p, 0, 0, 1), Wh(u, p, 0, 3, hme))
-            else:
-                recv(("G2", u, p, j, 1), Wp(u, p, j, 3))
-            ref = Wh(u, p, j, 3, hme)
-            send(("G2f", u, p, j, 1), ref, ref, near(1 - p, 1))
-            if j == 0:
-                recv(("G2", u, p, 0, 1, 3), Wh(u, p, 0, 1, oh))
-            else:
-                recv(("G2", u, p, j, 3), Wp(u, p, j, 1))
-            ref = Wh(u, p, j, 1, oh)
-            send(("G2f", u, p, j, 3), ref, ref, near(1 - p, 3))
+            ref = Wh(u, p, j, 3, i)
+            recv(("G2e", u, p, j), ref)
+            send(("G2f", u, p, j), ref, ref, near_w(1 - p, 1))
+        for p in range(2):
+            ahead(u, p, j)
+            ref = Wh(u, p, j, 1, i)
+            send(("G2m", u, p, (4 - j) % 4), ref, ref, zmir)
+
+    def ag2z(u, j):
+        for p in range(2):
+            ref = Wh(u, p, j, 2, i)
+            recv(("G2f", u, p, j), ref)
+            send(("G2z", u, p, (4 - j) % 4), ref, ref, zisl)
+
+    leaving = []
+
+    def leave(n, src, dst):
+        copy = pltpu.make_async_copy(src, dst, lsem.at[22 + n])
+        copy.start()
+        leaving.append(copy)
 
     seen = set()
 
@@ -315,14 +367,15 @@
         dy, dx = ARRIVAL[c]
         for p in range(2):
             ja, jb = (dx, dy) if p == 0 else (dy, dx)
-            if jb == 3 and ja == 0:
-                recv(("G2", u, p, 0, 1, 1), Wh(u, p, 0, 3, oh))
-            if jb == 1 and ja == 0:
-                recv(("G2", u, p, 0, 0, 3), Wh(u, p, 0, 1, hme))
+            if jb == 1:
+                ahead(u, p, ja)
+            if jb == 3:
+                recv(("G2e", u, p, ja), Wh(u, p, ja, 3, i))
+                recv(("G2m", u, p, ja), Wh(u, p, ja, 3, 1 - i))
             if jb == 2:
-                recv(("G2f", u, p, ja, 1), Wh(u, p, ja, 2, hme))
-                recv(("G2f", u, p, ja, 3), Wh(u, p, ja, 2, oh))
-        yy, xx = wrap(y + dy), wrap(x + dx)
+                recv(("G2f", u, p, ja), Wh(u, p, ja, 2, i))
+                recv(("G2z", u, p, ja), Wh(u, p, ja, 2, 1 - i))
+        yy, xx = wrap(y + sense * dy), wrap(x + sense * dx)
         right = W[u, yy, xx].reshape(512, 256)
         part = jnp.dot(Xc[yy * 4 + xx], right, preferred_element_type=f32)
         cols = slice(u * 256, (u + 1) * 256)
@@ -333,6 +386,7 @@
             acc[:, cols] += part
         else:
             out[:, cols] = ((acc[:, cols] + part) * D ** (-0.5)).astype(bf16)
+            leave(4 + u, out.at[:, cols], out_hbm.at[:, cols])
 
     for c in range(16):
         gradient(c)
@@ -356,41 +410,59 @@
     rs1c(1, 2)
     agz(0)
     rs1c(1, 1)
+    rs1c(1, 3)
     ag1(0)
-    rs1c(1, 3)
+    rs1c(1, 0)
+    rs2b(1)
     ag1f(0)
-    rs1c(1, 0)
     ag2f(0, 0)
-    rs2b(1)
+    rs2c(1)
     ag2f(0, 3)
-    rs2c(1)
     ag2f(0, 1)
     adam(1)
+    leave(0, nf, nf_hbm)
+    leave(1, ns, ns_hbm)
+    ag2z(0, 0)
     ag2f(0, 2)
     outer(1)
-    for c in range(0, 5):
+    leave(2, nm, nm_hbm)
+    leave(3, ng, ng_hbm)
+    ag2z(0, 3)
+    ag2z(0, 1)
+    for c in range(0, 3):
         project(0, c)
     agz(1)
-    for c in range(5, 9):
+    ag2z(0, 2)
+    for c in range(3, 6):
         project(0, c)
     ag1(1)
-    for c in range(9, 12):
+    for c in range(6, 10):
         project(0, c)
     ag1f(1)
-    for c in range(12, 16):
+    for c in range(10, 12):
         project(0, c)
     ag2f(1, 0)
+    for c in range(12, 14):
+        project(0, c)
+    ag2f(1, 3)
+    ag2f(1, 1)
+    for c in range(14, 16):
+        project(0, c)
+    ag2z(1, 0)
     project(1, 0)
+    ag2f(1, 2)
     project(1, 1)
-    ag2f(1, 3)
     project(1, 2)
+    ag2z(1, 3)
     project(1, 3)
-    ag2f(1, 1)
+    ag2z(1, 1)
     project(1, 4)
-    ag2f(1, 2)
+    ag2z(1, 2)
     for c in range(5, 16):
         project(1, c)
 
+    for copy in leaving:
+        copy.wait()
     for key, src, dst, to in sent:
         message(key, src, dst, to).wait_send()
     for c in range(16):
@@ -404,7 +476,20 @@
         raise ValueError(len(numbers.of))
 
 
-COUNT = 243
+COUNT = 255
+
+
+def hand_over(*refs):
+    ins, outs, held, sem = refs[:4], refs[4:8], refs[8:12], refs[12]
+    there = [pltpu.make_async_copy(a, b, sem.at[n]) for n, (a, b) in enumerate(zip(ins, held))]
+    back = [pltpu.make_async_copy(a, b, sem.at[4 + n]) for n, (a, b) in enumerate(zip(held, outs))]
+    for copy in there:
+        copy.start()
+    for first, second in zip(there, back):
+        first.wait()
+        second.start()
+    for copy in back:
+        copy.wait()
 
 
 def shards(
@@ -412,18 +497,20 @@
 ):
     tok, kv = cotangent.shape[0], cotangent.shape[2]
     rows = global_params.shape[0]
-    ct = cotangent.reshape(tok, 2 * kv).T
-    vmem = pl.BlockSpec(memory_space=pltpu.VMEM)
+    anywhere = pl.BlockSpec(memory_space=pl.ANY)
     state = jax.ShapeDtypeStruct((rows, 2, kv), f32)
-    import functools
-
     piece = (128, 256)
-    new_first, new_second, new_momentum, new_global, projected = pl.pallas_call(
+    held = pltpu.VMEM((rows, 2, kv), f32)
+    *states, projected = pl.pallas_call(
         functools.partial(kernel, COUNT),
         out_shape=(state, state, state, state, jax.ShapeDtypeStruct((tok, 2 * kv), bf16)),
-        in_specs=[pl.BlockSpec(memory_space=pl.ANY)] + [vmem] * 6,
-        out_specs=(vmem,) * 5,
+        in_specs=[anywhere] * 7,
+        out_specs=(anywhere,) * 5,
         scratch_shapes=[
+            pltpu.VMEM((tok, 2, kv), bf16),
+            pltpu.VMEM((2 * kv, tok), bf16),
+            held, held, held, held, held, held, held, held, held,
+            pltpu.VMEM((tok, 2 * kv), bf16),
             pltpu.VMEM((16, tok, 512), bf16),
             pltpu.VMEM((2, 2, 4, 4, 2) + piece, bf16),
             pltpu.VMEM((2, 2, 4, 2) + piece, bf16),
@@ -441,7 +528,7 @@
             pltpu.VMEM((2, 2, rows, kv // 2), bf16),
             pltpu.VMEM((2, 2, rows, kv // 2), bf16),
             pltpu.VMEM((tok, 2 * kv), f32),
-            pltpu.SemaphoreType.DMA((16,)),
+            pltpu.SemaphoreType.DMA((28,)),
             pltpu.SemaphoreType.DMA((COUNT,)),
             pltpu.SemaphoreType.DMA((COUNT,)),
         ],
@@ -453,9 +540,18 @@
         ),
         name="outer_step",
     )(
-        activations, ct, first_moment[0], second_moment[0], inner_params[0],
+        activations, cotangent, first_moment[0], second_moment[0], inner_params[0],
         global_params, outer_momentum,
     )
+    new_first, new_second, new_momentum, new_global = pl.pallas_call(
+        hand_over,
+        out_shape=(state,) * 4,
+        in_specs=[anywhere] * 4,
+        out_specs=(anywhere,) * 4,
+        scratch_shapes=[held] * 4 + [pltpu.SemaphoreType.DMA((8,))],
+        cost_estimate=pl.CostEstimate(flops=0, bytes_accessed=4 * 2**20, transcendentals=0),
+        name="hand_over",
+    )(*states)
     return (
         new_first[None], new_second[None], new_momentum, new_global,
         projected.reshape(tok, 2, kv),

time: 142 us -> 130 us (0.915)
  local copies, waits for them, and re-layouts: 13.8 us -> 2.14 us
    unnamed x5 -> x0, local copies, waits for them, and re-layouts: 11.7 us -> none
    pallas_call x0 -> x1, Pallas kernels: none -> 2.42 us  [shards(): pl.pallas_call(hand_over, out_shape=(state,) * 4, in_specs=[anywhere] * 4...]
    pallas_call x1, Pallas kernels: 127 us -> 125 us  [shards(): pl.pallas_call(functools.partial(kernel, COUNT), out_shape=(state, state,...]
where the time goes in v2:
time: 130 us
  Pallas kernels  127 us (98%)
  local copies, waits for them, and re-layouts  2.14 us (2%)
    pallas_call x1, Pallas kernels, shards(): pl.pallas_call(functools.partial(kernel, COUNT), out_shape=(state, state,...  125 us

profile of v2, /device:TPU:0, one launch (start us, length us, event | category | flops | bytes accessed | tf_op | source)
XLA Modules:
  0.0 130.2 jit_solution(3093359897405110092)
XLA Ops:
  0.6 125.0 %outer_step.1 = (f32[256,2,256]{2,1,0:T(2,128)}, f32[256,2,256]{2,1,0:T(2,128)}, f32[256,2,256]{2,1,0:T(2,128)}, f32[256,2,256]{2,1,0:T(2,128)}, bf16[1024,512]{1,0:T(8,128)(2,1)}) custom-call(bf16[1024,4096]{1,0:T(8,128)(2,1)} %x_hbm.1, bf16[1024,2,256]{2,1,0:T(2,128)(2,1)} %c_hbm.1, f32[256,2,256]{2,1,0:T(2,128)} %bitcast.5, f32[256,2,256]{2,1,0:T(2,128)} %bitcast.6, ...), custom_call_target="tpu_custom_call" | custom-call | flops 17200001024 | bytes 16777216 | tf_op jit(solution)/shard_map/outer_step/pallas_call | solution.py:504
  125.7 2.4 %hand_over.1 = (f32[256,2,256]{2,1,0:T(2,128)}, f32[256,2,256]{2,1,0:T(2,128)}, f32[256,2,256]{2,1,0:T(2,128)}, f32[256,2,256]{2,1,0:T(2,128)}) custom-call(f32[256,2,256]{2,1,0:T(2,128)} %get-tuple-element.14.refs_0_, f32[256,2,256]{2,1,0:T(2,128)} %get-tuple-element.15.refs_1_, f32[256,2,256]{2,1,0:T(2,128)} %get-tuple-element.16.refs_2_, ...), custom_call_target="tpu_custom_call" | custom-call | bytes 4194304 | tf_op jit(solution)/shard_map/hand_over/pallas_call | solution.py:546
  128.1 2.1 %reshape.13 = bf16[1024,2,256]{2,1,0:T(2,128)(2,1)} reshape(bf16[1024,512]{1,0:T(8,128)(2,1)} %get-tuple-element.22) | data formatting | bytes 2097152 | tf_op jit(solution)/shard_map/reshape | solution.py:557

commit v3 on v2

--- a/solution.py
+++ b/solution.py
@@ -31,6 +31,38 @@
 ]
 
 
+SCHEDULE = [
+    ("G", 0), ("S", 0, 0), ("G", 1), ("S", 0, 1), ("G", 2), ("S", 0, 2), ("G", 3), ("S", 0, 3), ("G", 4),
+    ("B", 0, 2, 1), ("S", 0, 4), ("Y", 0), ("S", 1, 0), ("G", 5), ("B", 0, 2, 0), ("G", 6), ("S", 0, 6),
+    ("S", 0, 5), ("G", 7), ("G", 8), ("S", 0, 7), ("S", 0, 8), ("B", 0, 1, 0), ("B", 0, 3, 1), ("G", 9),
+    ("S", 0, 9), ("B", 0, 1, 1), ("G", 10), ("C", 0, 2, 0), ("Y", 1), ("B", 0, 3, 0), ("G", 11), ("S", 1, 1),
+    ("C", 0, 2, 1), ("S", 0, 10), ("G", 12), ("G", 13), ("G", 14), ("S", 0, 13), ("C", 0, 3, 0), ("S", 0, 14),
+    ("C", 0, 1, 0), ("S", 0, 11), ("B", 0, 0, 0), ("T",), ("C", 0, 3, 1), ("C", 0, 1, 1), ("S", 0, 12),
+    ("Y", 2), ("Y", 3), ("B", 1, 2, 0), ("Y", 5), ("B", 0, 0, 1), ("S", 1, 3), ("Y", 4), ("Y", 11),
+    ("S", 1, 4), ("Y", 9), ("Y", 10), ("G", 15), ("S", 1, 2), ("Y", 6), ("B", 1, 2, 1), ("Y", 12),
+    ("S", 1, 10), ("C", 0, 0, 0), ("E", 0, 0), ("Y", 8), ("Y", 7), ("S", 1, 5), ("C", 0, 0, 1), ("S", 1, 6),
+    ("E", 0, 1), ("S", 1, 9), ("B", 1, 1, 1), ("Y", 13), ("Y", 14), ("S", 1, 8), ("S", 1, 7), ("B", 1, 3, 1),
+    ("B", 1, 3, 0), ("C", 1, 2, 0), ("B", 1, 1, 0), ("S", 1, 13), ("S", 1, 11), ("A", 0, 0), ("A", 0, 1),
+    ("C", 1, 2, 1), ("C", 1, 1, 1), ("S", 1, 12), ("B", 1, 0, 1), ("S", 1, 14), ("Y", 15), ("C", 1, 3, 1),
+    ("B", 1, 0, 0), ("C", 1, 3, 0), ("C", 1, 1, 0), ("O", 0), ("C", 1, 0, 1), ("E", 1, 1), ("C", 1, 0, 0),
+    ("E", 1, 0), ("Z", 0), ("K", 0, 0, 0), ("A", 1, 1), ("K", 0, 1, 0), ("A", 1, 0), ("I", 0, 1, 3),
+    ("I", 0, 0, 1), ("I", 0, 1, 1), ("I", 0, 0, 3), ("I", 0, 0, 2), ("I", 0, 1, 2), ("O", 1), ("K", 0, 1, 1),
+    ("M", 0, 1, 3), ("M", 0, 0, 1), ("K", 0, 0, 3), ("K", 0, 1, 2), ("N", 0, 1, 0), ("P", 0, 7),
+    ("N", 0, 0, 0), ("P", 0, 0), ("Z", 1), ("P", 0, 1), ("K", 0, 0, 2), ("M", 0, 1, 1), ("P", 0, 5),
+    ("K", 1, 0, 0), ("N", 0, 1, 1), ("M", 0, 0, 0), ("P", 0, 2), ("N", 0, 0, 3), ("K", 0, 1, 3),
+    ("I", 1, 1, 3), ("M", 0, 0, 3), ("K", 1, 1, 0), ("I", 1, 0, 3), ("N", 0, 1, 2), ("K", 0, 0, 1),
+    ("P", 0, 6), ("M", 0, 1, 0), ("P", 1, 0), ("M", 0, 1, 2), ("N", 0, 0, 2), ("P", 0, 8), ("N", 0, 1, 3),
+    ("I", 1, 1, 1), ("I", 1, 0, 1), ("M", 1, 0, 0), ("N", 1, 0, 0), ("I", 1, 0, 2), ("P", 1, 2),
+    ("K", 1, 1, 3), ("M", 0, 0, 2), ("I", 1, 1, 2), ("K", 1, 0, 3), ("M", 1, 1, 0), ("P", 0, 3),
+    ("N", 1, 1, 0), ("P", 0, 10), ("N", 0, 0, 1), ("P", 0, 15), ("K", 1, 1, 1), ("M", 1, 0, 3),
+    ("K", 1, 0, 1), ("M", 1, 1, 3), ("P", 1, 1), ("P", 0, 9), ("N", 1, 1, 3), ("P", 0, 4), ("P", 0, 12),
+    ("K", 1, 0, 2), ("N", 1, 0, 3), ("M", 1, 0, 1), ("P", 0, 11), ("P", 0, 13), ("N", 1, 1, 1),
+    ("N", 1, 0, 1), ("K", 1, 1, 2), ("P", 1, 4), ("M", 1, 1, 1), ("M", 1, 0, 2), ("P", 1, 5), ("M", 1, 1, 2),
+    ("P", 1, 3), ("N", 1, 0, 2), ("P", 1, 11), ("P", 0, 14), ("P", 1, 7), ("N", 1, 1, 2), ("P", 1, 12),
+    ("P", 1, 8), ("P", 1, 6), ("P", 1, 10), ("P", 1, 9), ("P", 1, 13), ("P", 1, 14), ("P", 1, 15),
+]
+
+
 class Numbers:
     def __init__(self):
         self.of = {}
@@ -43,7 +75,7 @@
     count, x_hbm, c_hbm, m_hbm, v_hbm, th_hbm, gp_hbm, om_hbm,
     nf_hbm, ns_hbm, nm_hbm, ng_hbm, out_hbm,
     cot, ct, m_ref, v_ref, th_ref, gp_ref, om_ref, nf, ns, nm, ng, out,
-    Xc, Pt, A2, Ap, Am, B2, Bp, Bm, Zs, Zr, F, W, Ts, Tr, As, Ar, acc,
+    Xc, Pt, Fs, Fr, A2, Ap, Am, B2, Bp, Bm, Zs, Zr, F, W, Ts, Tr, As, Ar, acc,
     lsem, ssem, rsem,
 ):
     i = lax.axis_index("island")
@@ -93,7 +125,7 @@
             message(key, dst, dst, peer).wait_recv()
 
     barrier = pltpu.get_barrier_semaphore()
-    friends = [near(0, 1), near(0, 3), near(1, 1), near(1, 3), peer, zfar, zisl, zmir]
+    friends = [near(a, g) for a in range(2) for g in (1, 2, 3)] + [peer, zfar, zisl, zmir]
     for d in friends:
         pl.semaphore_signal(barrier, inc=1, device_id=d, device_id_type=MESH)
 
@@ -157,78 +189,87 @@
             part = jnp.dot(
                 ct[...], Xc[k, :, h * 256 : (h + 1) * 256], preferred_element_type=f32
             ).astype(bf16)
-            for u in range(2):
-                for p in range(2):
-                    r = (u * 2 + p) * 128
-                    Pt[u, p, yy, xx, h] = part[r : r + 128]
+            for p in range(2):
+                r = p * 128
+                Pt[0, p, yy, xx, h] = part[r : r + 128]
+                r = 256 + p * 128
+                Pt[1, p, yy, xx, h, 0:64] = part[r : r + 64]
+                Fs[yy, xx, h, p] = part[r + 64 : r + 128]
+        send(("F", c), Fs.at[yy, xx, oh], Fr.at[yy, xx], zfar)
+
+    def fold(c):
+        dy, dx = ORDER[c]
+        yy, xx = wrap(y + dy), wrap(x + dx)
+        recv(("F", c), Fr.at[yy, xx])
+        for p in range(2):
+            total = (Fs[yy, xx, hme, p].astype(f32) + Fr[yy, xx, p].astype(f32)).astype(bf16)
+            for h in range(2):
+                Pt[1, p, yy, xx, h, 64:96] = total[32 * h : 32 * h + 32]
+
+    def cut(u):
+        return pl.ds(0, 128 if u == 0 else 96)
 
     def Pc(u, p, ja, jb, h):
         yy, xx = place(p, ja, jb)
-        return Pt.at[u, p, yy, xx, h]
+        return Pt.at[u, p, yy, xx, h, cut(u)]
+
+    def Pb(u, p, ja, jb):
+        yy, xx = place(p, ja, jb)
+        return Pt.at[u, p, yy, xx, :, cut(u)]
+
+    def slot(ref, u, p, jb, h):
+        return ref.at[u, p, jb, h, cut(u)]
 
     def first_sends(u, c):
         dy, dx = ORDER[c]
         for p in range(2):
-            a = p
             ja, jb = (dx, dy) if p == 0 else (dy, dx)
             if ja == 2:
-                send(("A2", u, p, jb, 0), Pc(u, p, 2, jb, 0), A2.at[u, p, jb, 0], near(a, 1))
-                send(("A2", u, p, jb, 1), Pc(u, p, 2, jb, 1), A2.at[u, p, jb, 1], near(a, 3))
+                send(("A2", u, p, jb, 0), Pc(u, p, 2, jb, 0), slot(A2, u, p, jb, 0), near(p, 1))
+                send(("A2", u, p, jb, 1), Pc(u, p, 2, jb, 1), slot(A2, u, p, jb, 1), near(p, 3))
             elif ja == 1:
-                send(("Am", u, p, jb, 1), Pc(u, p, 1, jb, 1), Am.at[u, p, jb, 1], near(a, 1))
+                send(("Am", u, p, jb, 1), Pc(u, p, 1, jb, 1), slot(Am, u, p, jb, 1), near(p, 1))
             elif ja == 3:
-                send(("Ap", u, p, jb, 0), Pc(u, p, 3, jb, 0), Ap.at[u, p, jb, 0], near(a, 3))
+                send(("Ap", u, p, jb, 0), Pc(u, p, 3, jb, 0), slot(Ap, u, p, jb, 0), near(p, 3))
 
     def add_to(dst, src):
         dst[...] = (dst[...].astype(f32) + src[...].astype(f32)).astype(bf16)
 
-    def rs1b(u, jb):
-        for p in range(2):
-            a = p
-            recv(("A2", u, p, jb, 0), A2.at[u, p, jb, 0])
-            add_to(Pc(u, p, 1, jb, 0), A2.at[u, p, jb, 0])
-            send(("Am", u, p, jb, 0), Pc(u, p, 1, jb, 0), Am.at[u, p, jb, 0], near(a, 1))
-            recv(("A2", u, p, jb, 1), A2.at[u, p, jb, 1])
-            add_to(Pc(u, p, 3, jb, 1), A2.at[u, p, jb, 1])
-            send(("Ap", u, p, jb, 1), Pc(u, p, 3, jb, 1), Ap.at[u, p, jb, 1], near(a, 3))
-
-    def rs1c(u, jb):
-        for p in range(2):
-            b = 1 - p
-            for h in range(2):
-                recv(("Am", u, p, jb, h), Am.at[u, p, jb, h])
-                recv(("Ap", u, p, jb, h), Ap.at[u, p, jb, h])
-                own = Pc(u, p, 0, jb, h)
-                s = own[...].astype(f32) + Am[u, p, jb, h].astype(f32) + Ap[u, p, jb, h].astype(f32)
-                if jb == 0:
-                    F[u, p, h] = s
-                else:
-                    own[...] = s.astype(bf16)
-                    if jb == 2:
-                        send(("B2", u, p, h), own, B2.at[u, p, h], near(b, 1 if h == 0 else 3))
-                    elif jb == 1 and h == 1:
-                        send(("Bm", u, p, 1), own, Bm.at[u, p, 1], near(b, 1))
-                    elif jb == 3 and h == 0:
-                        send(("Bp", u, p, 0), own, Bp.at[u, p, 0], near(b, 3))
-
-    def rs2b(u):
-        for p in range(2):
-            b = 1 - p
-            recv(("B2", u, p, 0), B2.at[u, p, 0])
-            add_to(Pc(u, p, 0, 1, 0), B2.at[u, p, 0])
-            send(("Bm", u, p, 0), Pc(u, p, 0, 1, 0), Bm.at[u, p, 0], near(b, 1))
-            recv(("B2", u, p, 1), B2.at[u, p, 1])
-            add_to(Pc(u, p, 0, 3, 1), B2.at[u, p, 1])
-            send(("Bp", u, p, 1), Pc(u, p, 0, 3, 1), Bp.at[u, p, 1], near(b, 3))
-
-    def rs2c(u):
-        for p in range(2):
-            for h in range(2):
-                recv(("Bm", u, p, h), Bm.at[u, p, h])
-                recv(("Bp", u, p, h), Bp.at[u, p, h])
-                F[u, p, h] += Bm[u, p, h].astype(f32) + Bp[u, p, h].astype(f32)
-            Zs[u, p] = F[u, p, oh].astype(bf16)
-            send(("Z", u, p), Zs.at[u, p], Zr.at[u, p], zfar)
+    def middle(u, jb, p):
+        own, far = Pc(u, p, 1, jb, 0), slot(A2, u, p, jb, 0)
+        recv(("A2", u, p, jb, 0), far)
+        add_to(own, far)
+        send(("Am", u, p, jb, 0), own, slot(Am, u, p, jb, 0), near(p, 1))
+        own, far = Pc(u, p, 3, jb, 1), slot(A2, u, p, jb, 1)
+        recv(("A2", u, p, jb, 1), far)
+        add_to(own, far)
+        send(("Ap", u, p, jb, 1), own, slot(Ap, u, p, jb, 1), near(p, 3))
+
+    def close(u, jb, p):
+        for h in range(2):
+            below, above = slot(Am, u, p, jb, h), slot(Ap, u, p, jb, h)
+            recv(("Am", u, p, jb, h), below)
+            recv(("Ap", u, p, jb, h), above)
+            own = Pc(u, p, 0, jb, h)
+            total = own[...].astype(f32) + below[...].astype(f32) + above[...].astype(f32)
+            if jb == 0:
+                F[u, p, h, cut(u)] = total
+            else:
+                own[...] = total.astype(bf16)
+        if jb != 0:
+            name, ref = {1: ("Bm", Bm), 2: ("B2", B2), 3: ("Bp", Bp)}[jb]
+            send((name, u, p), Pb(u, p, 0, jb), ref.at[u, p, :, cut(u)], near(1 - p, jb))
+
+    def second(u, p):
+        refs = [ref.at[u, p, :, cut(u)] for ref in (Bm, Bp, B2)]
+        for name, ref in zip(("Bm", "Bp", "B2"), refs):
+            recv((name, u, p), ref)
+        for h in range(2):
+            more = [ref[u, p, h, cut(u)].astype(f32) for ref in (Bm, Bp, B2)]
+            F[u, p, h, cut(u)] = F[u, p, h, cut(u)] + (more[0] + more[1] + more[2])
+        n = pl.ds(0, 128 if u == 0 else 64)
+        Zs[u, p, n] = F[u, p, oh, n].astype(bf16)
+        send(("Z", u, p), Zs.at[u, p, n], Zr.at[u, p, n], zfar)
 
     def start_islands():
         for copy in state_in[1:]:
@@ -238,21 +279,24 @@
             Ts[u] = gp_ref[:, u, :] - (th - (inner_rate * weight_decay) * th)
         send(("T",), Ts, Tr, zisl)
 
-    def adam(u):
-        for p in range(2):
-            cols = slice(p * 128, (p + 1) * 128)
-            recv(("Z", u, p), Zr.at[u, p])
-            grad = (F[u, p, hme] + Zr[u, p].astype(f32)).T
-            first = beta_one * m_ref[:, u, cols] + (1.0 - beta_one) * grad
-            second = beta_two * v_ref[:, u, cols] + (1.0 - beta_two) * grad * grad
-            nf[:, u, cols] = first
-            ns[:, u, cols] = second
-            ascent = (
-                first / (1.0 - beta_one**STEP)
-                / (jnp.sqrt(second / (1.0 - beta_two**STEP)) + adam_eps)
-            )
-            As[u, p] = ascent.astype(bf16)
-            send(("I", u, p), As.at[u, p], Ar.at[u, p], zisl)
+    def adam(u, p):
+        cols = slice(p * 128, (p + 1) * 128)
+        n = pl.ds(0, 128 if u == 0 else 64)
+        recv(("Z", u, p), Zr.at[u, p, n])
+        total = F[u, p, hme, n] + Zr[u, p, n].astype(f32)
+        if u == 1:
+            total = jnp.concatenate([total, F[u, p, 0, 64:96], F[u, p, 1, 64:96]], axis=0)
+        grad = total.T
+        first = beta_one * m_ref[:, u, cols] + (1.0 - beta_one) * grad
+        second = beta_two * v_ref[:, u, cols] + (1.0 - beta_two) * grad * grad
+        nf[:, u, cols] = first
+        ns[:, u, cols] = second
+        ascent = (
+            first / (1.0 - beta_one**STEP)
+            / (jnp.sqrt(second / (1.0 - beta_two**STEP)) + adam_eps)
+        )
+        As[u, p] = ascent.astype(bf16)
+        send(("I", u, p), As.at[u, p], Ar.at[u, p], zisl)
 
     def place_w(p, ja, jb):
         return place(p, sense * ja, sense * jb)
@@ -289,7 +333,7 @@
         h = hme if s == 0 else oh
         for p in range(2):
             ref = Wh(u, p, 0, 0, h)
-            for g in (1, 3):
+            for g in (1, 3, 2):
                 send(("G1", u, p, s, g), ref, ref, near_w(p, g))
             send(("G2b", u, p, 0, s), ref, ref, near_w(1 - p, 3))
 
@@ -311,25 +355,10 @@
         ref = Wp(u, p, j, 0)
         send(("G2b", u, p, j), ref, ref, near_w(1 - p, 3))
 
-    def ag1(u):
-        for p in range(2):
-            ref = Wh(u, p, 3, 0, hme)
-            recv(("G1", u, p, 0, 1), ref)
-            send(("G1f", u, p, 1), ref, ref, near_w(p, 1))
-            ref = Wh(u, p, 1, 0, oh)
-            recv(("G1", u, p, 1, 3), ref)
-            send(("G1f", u, p, 3), ref, ref, near_w(p, 3))
-        for p in range(2):
-            recv(("G1", u, p, 1, 1), Wh(u, p, 3, 0, oh))
-            g2(u, p, 3)
-            recv(("G1", u, p, 0, 3), Wh(u, p, 1, 0, hme))
-            g2(u, p, 1)
-
-    def ag1f(u):
-        for p in range(2):
-            recv(("G1f", u, p, 1), Wh(u, p, 2, 0, hme))
-            recv(("G1f", u, p, 3), Wh(u, p, 2, 0, oh))
-            g2(u, p, 2)
+    def pass_on(u, p, j):
+        recv(("G1", u, p, 0, 4 - j), Wh(u, p, j, 0, hme))
+        recv(("G1", u, p, 1, 4 - j), Wh(u, p, j, 0, oh))
+        g2(u, p, j)
 
     def ahead(u, p, j):
         if j == 0:
@@ -338,21 +367,20 @@
         else:
             recv(("G2b", u, p, j), Wp(u, p, j, 1))
 
-    def ag2f(u, j):
-        for p in range(2):
-            ref = Wh(u, p, j, 3, i)
-            recv(("G2e", u, p, j), ref)
-            send(("G2f", u, p, j), ref, ref, near_w(1 - p, 1))
-        for p in range(2):
-            ahead(u, p, j)
-            ref = Wh(u, p, j, 1, i)
-            send(("G2m", u, p, (4 - j) % 4), ref, ref, zmir)
-
-    def ag2z(u, j):
-        for p in range(2):
-            ref = Wh(u, p, j, 2, i)
-            recv(("G2f", u, p, j), ref)
-            send(("G2z", u, p, (4 - j) % 4), ref, ref, zisl)
+    def onward(u, p, j):
+        ref = Wh(u, p, j, 3, i)
+        recv(("G2e", u, p, j), ref)
+        send(("G2f", u, p, j), ref, ref, near_w(1 - p, 1))
+
+    def to_mirror(u, p, j):
+        ahead(u, p, j)
+        ref = Wh(u, p, j, 1, i)
+        send(("G2m", u, p, (4 - j) % 4), ref, ref, zmir)
+
+    def to_island(u, p, j):
+        ref = Wh(u, p, j, 2, i)
+        recv(("G2f", u, p, j), ref)
+        send(("G2z", u, p, (4 - j) % 4), ref, ref, zisl)
 
     leaving = []
 
@@ -361,7 +389,7 @@
         copy.start()
         leaving.append(copy)
 
-    seen = set()
+    seen = {0: 0, 1: 0}
 
     def project(u, c):
         dy, dx = ARRIVAL[c]
@@ -379,87 +407,30 @@
         right = W[u, yy, xx].reshape(512, 256)
         part = jnp.dot(Xc[yy * 4 + xx], right, preferred_element_type=f32)
         cols = slice(u * 256, (u + 1) * 256)
-        if u not in seen:
-            seen.add(u)
+        seen[u] += 1
+        if seen[u] == 1:
             acc[:, cols] = part
-        elif c < 15:
+        elif seen[u] < 16:
             acc[:, cols] += part
         else:
             out[:, cols] = ((acc[:, cols] + part) * D ** (-0.5)).astype(bf16)
             leave(4 + u, out.at[:, cols], out_hbm.at[:, cols])
 
-    for c in range(16):
-        gradient(c)
-        first_sends(0, c)
-        if c == 6:
-            start_islands()
-    for q, jb in enumerate((2, 1, 3, 0)):
-        rs1b(0, jb)
-        for c in range(4 * q, 4 * q + 4):
-            first_sends(1, c)
-    for jb in (2, 1, 3, 0):
-        rs1c(0, jb)
-    rs2b(0)
-    rs1b(1, 2)
-    rs2c(0)
-    rs1b(1, 1)
-    adam(0)
-    rs1b(1, 3)
-    rs1b(1, 0)
-    outer(0)
-    rs1c(1, 2)
-    agz(0)
-    rs1c(1, 1)
-    rs1c(1, 3)
-    ag1(0)
-    rs1c(1, 0)
-    rs2b(1)
-    ag1f(0)
-    ag2f(0, 0)
-    rs2c(1)
-    ag2f(0, 3)
-    ag2f(0, 1)
-    adam(1)
-    leave(0, nf, nf_hbm)
-    leave(1, ns, ns_hbm)
-    ag2z(0, 0)
-    ag2f(0, 2)
-    outer(1)
-    leave(2, nm, nm_hbm)
-    leave(3, ng, ng_hbm)
-    ag2z(0, 3)
-    ag2z(0, 1)
-    for c in range(0, 3):
-        project(0, c)
-    agz(1)
-    ag2z(0, 2)
-    for c in range(3, 6):
-        project(0, c)
-    ag1(1)
-    for c in range(6, 10):
-        project(0, c)
-    ag1f(1)
-    for c in range(10, 12):
-        project(0, c)
-    ag2f(1, 0)
-    for c in range(12, 14):
-        project(0, c)
-    ag2f(1, 3)
-    ag2f(1, 1)
-    for c in range(14, 16):
-        project(0, c)
-    ag2z(1, 0)
-    project(1, 0)
-    ag2f(1, 2)
-    project(1, 1)
-    project(1, 2)
-    ag2z(1, 3)
-    project(1, 3)
-    ag2z(1, 1)
-    project(1, 4)
-    ag2z(1, 2)
-    for c in range(5, 16):
-        project(1, c)
+    steps = {
+        "G": gradient, "Y": fold, "T": start_islands, "S": first_sends, "B": middle, "C": close,
+        "E": second, "A": adam, "O": outer, "Z": agz, "I": pass_on, "K": onward,
+        "M": to_mirror, "N": to_island, "P": project,
+    }
+    counts = {}
+    for name, *where in SCHEDULE:
+        steps[name](*where)
+        counts[name] = counts.get(name, 0) + 1
+        if name == "A" and counts[name] == 4:
+            leave(0, nf, nf_hbm)
+            leave(1, ns, ns_hbm)
+        if name == "O" and counts[name] == 2:
+            leave(2, nm, nm_hbm)
+            leave(3, ng, ng_hbm)
 
     for copy in leaving:
         copy.wait()
@@ -476,7 +447,7 @@
         raise ValueError(len(numbers.of))
 
 
-COUNT = 255
+COUNT = 259
 
 
 def hand_over(*refs):
@@ -513,6 +484,8 @@
             pltpu.VMEM((tok, 2 * kv), bf16),
             pltpu.VMEM((16, tok, 512), bf16),
             pltpu.VMEM((2, 2, 4, 4, 2) + piece, bf16),
+            pltpu.VMEM((4, 4, 2, 2, 64, 256), bf16),
+            pltpu.VMEM((4, 4, 2, 64, 256), bf16),
             pltpu.VMEM((2, 2, 4, 2) + piece, bf16),
             pltpu.VMEM((2, 2, 4, 2) + piece, bf16),
             pltpu.VMEM((2, 2, 4, 2) + piece, bf16),

time: 130 us -> 113 us (0.87)
  Pallas kernels: 127 us -> 110 us
    pallas_call x1, Pallas kernels: 125 us -> 107 us  [shards(): pl.pallas_call(functools.partial(kernel, COUNT), out_shape=(state, state,...]
where the time goes in v3:
time: 113 us; the launch traced here: 112 us
  Pallas kernels  110 us (97%)
  local copies, waits for them, and re-layouts  2.14 us (2%)
    pallas_call x1, Pallas kernels, shards(): pl.pallas_call(functools.partial(kernel, COUNT), out_shape=(state, state,...  107 us
    pallas_call x1, Pallas kernels, shards(): pl.pallas_call(hand_over, out_shape=(state,) * 4, in_specs=[anywhere] * 4...  2.42 us

profile of v3, /device:TPU:0, one launch (start us, length us, event | category | flops | bytes accessed | tf_op | source)
XLA Modules:
  0.0 112.5 jit_solution(10887830630630239066)
XLA Ops:
  0.6 107.2 %outer_step.1 = (f32[256,2,256]{2,1,0:T(2,128)}, f32[256,2,256]{2,1,0:T(2,128)}, f32[256,2,256]{2,1,0:T(2,128)}, f32[256,2,256]{2,1,0:T(2,128)}, bf16[1024,512]{1,0:T(8,128)(2,1)}) custom-call(bf16[1024,4096]{1,0:T(8,128)(2,1)} %x_hbm.1, bf16[1024,2,256]{2,1,0:T(2,128)(2,1)} %c_hbm.1, f32[256,2,256]{2,1,0:T(2,128)} %bitcast.5, f32[256,2,256]{2,1,0:T(2,128)} %bitcast.6, ...), custom_call_target="tpu_custom_call" | custom-call | flops 17200001024 | bytes 16777216 | tf_op jit(solution)/shard_map/outer_step/pallas_call | solution.py:475
  107.9 2.4 %hand_over.1 = (f32[256,2,256]{2,1,0:T(2,128)}, f32[256,2,256]{2,1,0:T(2,128)}, f32[256,2,256]{2,1,0:T(2,128)}, f32[256,2,256]{2,1,0:T(2,128)}) custom-call(f32[256,2,256]{2,1,0:T(2,128)} %get-tuple-element.14.refs_0_, f32[256,2,256]{2,1,0:T(2,128)} %get-tuple-element.15.refs_1_, f32[256,2,256]{2,1,0:T(2,128)} %get-tuple-element.16.refs_2_, ...), custom_call_target="tpu_custom_call" | custom-call | bytes 4194304 | tf_op jit(solution)/shard_map/hand_over/pallas_call | solution.py:519
  110.3 2.1 %reshape.13 = bf16[1024,2,256]{2,1,0:T(2,128)(2,1)} reshape(bf16[1024,512]{1,0:T(8,128)(2,1)} %get-tuple-element.22) | data formatting | bytes 2097152 | tf_op jit(solution)/shard_map/reshape | solution.py:530

commit v4 on v3

--- a/solution.py
+++ b/solution.py
@@ -36,7 +36,7 @@
     ("B", 0, 2, 1), ("S", 0, 4), ("Y", 0), ("S", 1, 0), ("G", 5), ("B", 0, 2, 0), ("G", 6), ("S", 0, 6),
     ("S", 0, 5), ("G", 7), ("G", 8), ("S", 0, 7), ("S", 0, 8), ("B", 0, 1, 0), ("B", 0, 3, 1), ("G", 9),
     ("S", 0, 9), ("B", 0, 1, 1), ("G", 10), ("C", 0, 2, 0), ("Y", 1), ("B", 0, 3, 0), ("G", 11), ("S", 1, 1),
-    ("C", 0, 2, 1), ("S", 0, 10), ("G", 12), ("G", 13), ("G", 14), ("S", 0, 13), ("C", 0, 3, 0), ("S", 0, 14),
+    ("C", 0, 2, 1), ("S", 0, 10), ("R",), ("G", 12), ("G", 13), ("G", 14), ("S", 0, 13), ("C", 0, 3, 0), ("S", 0, 14),
     ("C", 0, 1, 0), ("S", 0, 11), ("B", 0, 0, 0), ("T",), ("C", 0, 3, 1), ("C", 0, 1, 1), ("S", 0, 12),
     ("Y", 2), ("Y", 3), ("B", 1, 2, 0), ("Y", 5), ("B", 0, 0, 1), ("S", 1, 3), ("Y", 4), ("Y", 11),
     ("S", 1, 4), ("Y", 9), ("Y", 10), ("G", 15), ("S", 1, 2), ("Y", 6), ("B", 1, 2, 1), ("Y", 12),
@@ -75,7 +75,7 @@
     count, x_hbm, c_hbm, m_hbm, v_hbm, th_hbm, gp_hbm, om_hbm,
     nf_hbm, ns_hbm, nm_hbm, ng_hbm, out_hbm,
     cot, ct, m_ref, v_ref, th_ref, gp_ref, om_ref, nf, ns, nm, ng, out,
-    Xc, Pt, Fs, Fr, A2, Ap, Am, B2, Bp, Bm, Zs, Zr, F, W, Ts, Tr, As, Ar, acc,
+    Xc, Pt, Fs, Fr, A2, Ap, Am, B2, Bp, Bm, Zs, Zr, F, W, Ts, Tr, As, Ar, acc, Ms, Vs, Gs, Os,
     lsem, ssem, rsem,
 ):
     i = lax.axis_index("island")
@@ -159,10 +159,6 @@
 
     for copy in state_in[1:]:
         copy.start()
-    state_in[0].wait()
-    for u in range(2):
-        ct[u * 256 : (u + 1) * 256, :] = cot[:, u, :].T
-
     pl.semaphore_wait(barrier, len(friends))
     for c in range(16):
         k, mine, src = chunk(c)
@@ -171,6 +167,10 @@
         @pl.when(mine)
         def _():
             message(("X", c), src, Xc.at[k], peer).start()
+
+    state_in[0].wait()
+    for u in range(2):
+        ct[u * 256 : (u + 1) * 256, :] = cot[:, u, :].T
 
     def gradient(c):
         k, mine, src = chunk(c)
@@ -272,12 +272,18 @@
         send(("Z", u, p), Zs.at[u, p, n], Zr.at[u, p, n], zfar)
 
     def start_islands():
-        for copy in state_in[1:]:
-            copy.wait()
+        state_in[1].wait()
         for u in range(2):
             th = th_ref[:, u, :]
             Ts[u] = gp_ref[:, u, :] - (th - (inner_rate * weight_decay) * th)
         send(("T",), Ts, Tr, zisl)
+
+    def plain_states():
+        for copy in state_in[2:]:
+            copy.wait()
+        for u in range(2):
+            for flat, ref in ((Ms, m_ref), (Vs, v_ref), (Gs, gp_ref), (Os, om_ref)):
+                flat[u] = ref[:, u, :]
 
     def adam(u, p):
         cols = slice(p * 128, (p + 1) * 128)
@@ -287,16 +293,16 @@
         if u == 1:
             total = jnp.concatenate([total, F[u, p, 0, 64:96], F[u, p, 1, 64:96]], axis=0)
         grad = total.T
-        first = beta_one * m_ref[:, u, cols] + (1.0 - beta_one) * grad
-        second = beta_two * v_ref[:, u, cols] + (1.0 - beta_two) * grad * grad
-        nf[:, u, cols] = first
-        ns[:, u, cols] = second
+        first = beta_one * Ms[u, :, cols] + (1.0 - beta_one) * grad
+        second = beta_two * Vs[u, :, cols] + (1.0 - beta_two) * grad * grad
         ascent = (
             first / (1.0 - beta_one**STEP)
             / (jnp.sqrt(second / (1.0 - beta_two**STEP)) + adam_eps)
         )
         As[u, p] = ascent.astype(bf16)
         send(("I", u, p), As.at[u, p], Ar.at[u, p], zisl)
+        nf[:, u, cols] = first
+        ns[:, u, cols] = second
 
     def place_w(p, ja, jb):
         return place(p, sense * ja, sense * jb)
@@ -314,20 +320,23 @@
 
     def outer(u):
         recv(("T",), Tr)
+        results = []
         for p in range(2):
             cols = slice(p * 128, (p + 1) * 128)
             recv(("I", u, p), Ar.at[u, p])
             steps = As[u, p].astype(f32) + Ar[u, p].astype(f32)
             delta = ((Ts[u, :, cols] + Tr[u, :, cols]) + inner_rate * steps) * 0.5
-            momentum = outer_mu * om_ref[:, u, cols] + delta
-            fresh = gp_ref[:, u, cols] - outer_rate * (delta + outer_mu * momentum)
-            nm[:, u, cols] = momentum
-            ng[:, u, cols] = fresh
+            momentum = outer_mu * Os[u, :, cols] + delta
+            fresh = Gs[u, :, cols] - outer_rate * (delta + outer_mu * momentum)
+            results.append((cols, momentum, fresh))
             low = fresh.astype(bf16)
             W[u, y, x, hme, 0, :, cols] = low[:128]
             W[u, y, x, hme, 1, :, cols] = low[128:]
         send(("Gz", u), W.at[u, y, x, hme], W.at[u, y, x, hme], zmir)
         spread(u, 0)
+        for cols, momentum, fresh in results:
+            nm[:, u, cols] = momentum
+            ng[:, u, cols] = fresh
 
     def spread(u, s):
         h = hme if s == 0 else oh
@@ -417,7 +426,7 @@
             leave(4 + u, out.at[:, cols], out_hbm.at[:, cols])
 
     steps = {
-        "G": gradient, "Y": fold, "T": start_islands, "S": first_sends, "B": middle, "C": close,
+        "G": gradient, "Y": fold, "T": start_islands, "R": plain_states, "S": first_sends, "B": middle, "C": close,
         "E": second, "A": adam, "O": outer, "Z": agz, "I": pass_on, "K": onward,
         "M": to_mirror, "N": to_island, "P": project,
     }
@@ -501,6 +510,10 @@
             pltpu.VMEM((2, 2, rows, kv // 2), bf16),
             pltpu.VMEM((2, 2, rows, kv // 2), bf16),
             pltpu.VMEM((tok, 2 * kv), f32),
+            pltpu.VMEM((2, rows, kv), f32),
+            pltpu.VMEM((2, rows, kv), f32),
+            pltpu.VMEM((2, rows, kv), f32),
+            pltpu.VMEM((2, rows, kv), f32),
             pltpu.SemaphoreType.DMA((28,)),
             pltpu.SemaphoreType.DMA((COUNT,)),
             pltpu.SemaphoreType.DMA((COUNT,)),

time: 113 us -> 112 us (level)
  no operation moved by 1% of the time
where the time goes in v4:
time: 112 us
  Pallas kernels  109 us (97%)
  local copies, waits for them, and re-layouts  2.14 us (2%)
    pallas_call x1, Pallas kernels, shards(): pl.pallas_call(functools.partial(kernel, COUNT), out_shape=(state, state,...  107 us
    pallas_call x1, Pallas kernels, shards(): pl.pallas_call(hand_over, out_shape=(state,) * 4, in_specs=[anywhere] * 4...  2.42 us

profile of v4, /device:TPU:0, one launch (start us, length us, event | category | flops | bytes accessed | tf_op | source)
XLA Modules:
  0.0 111.9 jit_solution(3992074484093016629)
XLA Ops:
  0.6 106.7 %outer_step.1 = (f32[256,2,256]{2,1,0:T(2,128)}, f32[256,2,256]{2,1,0:T(2,128)}, f32[256,2,256]{2,1,0:T(2,128)}, f32[256,2,256]{2,1,0:T(2,128)}, bf16[1024,512]{1,0:T(8,128)(2,1)}) custom-call(bf16[1024,4096]{1,0:T(8,128)(2,1)} %x_hbm.1, bf16[1024,2,256]{2,1,0:T(2,128)(2,1)} %c_hbm.1, f32[256,2,256]{2,1,0:T(2,128)} %bitcast.5, f32[256,2,256]{2,1,0:T(2,128)} %bitcast.6, ...), custom_call_target="tpu_custom_call" | custom-call | flops 17200001024 | bytes 16777216 | tf_op jit(solution)/shard_map/outer_step/pallas_call | solution.py:484
  107.3 2.4 %hand_over.1 = (f32[256,2,256]{2,1,0:T(2,128)}, f32[256,2,256]{2,1,0:T(2,128)}, f32[256,2,256]{2,1,0:T(2,128)}, f32[256,2,256]{2,1,0:T(2,128)}) custom-call(f32[256,2,256]{2,1,0:T(2,128)} %get-tuple-element.14.refs_0_, f32[256,2,256]{2,1,0:T(2,128)} %get-tuple-element.15.refs_1_, f32[256,2,256]{2,1,0:T(2,128)} %get-tuple-element.16.refs_2_, ...), custom_call_target="tpu_custom_call" | custom-call | bytes 4194304 | tf_op jit(solution)/shard_map/hand_over/pallas_call | solution.py:532
  109.8 2.1 %reshape.13 = bf16[1024,2,256]{2,1,0:T(2,128)(2,1)} reshape(bf16[1024,512]{1,0:T(8,128)(2,1)} %get-tuple-element.22) | data formatting | bytes 2097152 | tf_op jit(solution)/shard_map/reshape | solution.py:543
